TPU v7x, 256 devices: a whole 4x4x8 slice. The times are simulated.
256 devices in a mesh: row: 32 (over y, z_hi, core), col: 8 (over x, z_lo).
Axes of the slice: x: 4, y: 4, z: 8 (z_hi: 4, z_lo: 2; z = z_hi * 2 + z_lo), core: 2. Of those that a mesh axis runs over, the one named last changes fastest.
Arguments:
- blocks: bfloat16 [65536, 4096], P('row', 'col'), may hold values from -0.046875 to 0.046875
- factors: float32 [128, 512, 512], P('row'), as said below
- block_live: int32 [128], P('row'), may hold values from 1 to 512, 49152 in all
Outputs:
- schur_matrix: float32 [4096, 4096], P('row', 'col')
- panel_factor: float32 [4096, 512], P('row', 'col')
Inputs may be any that keep to these rules, and one draw needn't show every extreme that they name: `factors`: each block is lower triangular with a positive diagonal and zeros above it. `block_live`: rows of a block at or beyond its count are left out.
All inputs are finite; a program needn't handle non-finite values.
Results may differ from a plain program's by a relative error of at most 0.0014.
Values may be sent and summed in bfloat16 or wider, within the bound.
A program may use at most 128 MiB of HBM per device.

v0:
```python
import jax
import jax.numpy as jnp
from jax import lax
from jax.sharding import Mesh
from jax.sharding import PartitionSpec as P

LEAD = 512
COL = ("col_0", "col_1")


def gathered_by_axis(value, axes, dim):
    if not axes:
        return value
    nearer = lax.all_gather(value, axes[-1], axis=dim, tiled=True)
    return gathered_by_axis(nearer, axes[:-1], dim)


def picked_2(value, axis, root):
    return lax.dynamic_index_in_dim(lax.all_gather(value, axis), root, 0, keepdims=False)


def whiten(segment, factors, block_live):
    count_blocks = factors.shape[0]
    order = factors.shape[1]
    columns = segment.shape[1]
    shaped = segment.reshape(count_blocks, order, columns).astype(jnp.float32)
    solved = jax.vmap(
        lambda factor, right: jax.scipy.linalg.solve_triangular(factor, right, lower=True)
    )(factors, shaped)
    row_index = jnp.arange(order, dtype=jnp.int32)
    solved = jnp.where(row_index[None, :, None] < block_live[:, None, None], solved, 0.0)
    return solved.reshape(count_blocks * order, columns).astype(jnp.bfloat16)


def body(blocks, factors, block_live):
    own_panel = whiten(blocks, factors, block_live)
    gathered = gathered_by_axis(own_panel, COL, 1)
    all_columns = gathered.shape[1]
    slab_rows = all_columns // lax.axis_size("row")
    schur_slab = lax.psum_scatter(
        lax.dot_general(
            gathered, own_panel, (((0,), (0,)), ((), ())), preferred_element_type=jnp.float32
        ),
        "row",
        scatter_dimension=0,
        tiled=True,
    )
    leading_cols = picked_2(schur_slab, COL, 0)
    pieces = []
    for source in range(LEAD // slab_rows):
        pieces.append(picked_2(leading_cols, "row", source))
    leading_block = jnp.concatenate(pieces, axis=0)
    lead_factor = jnp.linalg.cholesky(leading_block)
    lead_inverse = jax.scipy.linalg.solve_triangular(
        lead_factor, jnp.eye(LEAD, dtype=jnp.float32), lower=True
    )
    out_width = LEAD // lax.axis_size(COL)
    inverse_rows = lax.dynamic_slice_in_dim(
        lead_inverse, lax.axis_index(COL) * out_width, out_width, 0
    )
    panel_factor = jnp.dot(leading_cols, inverse_rows.T, precision=lax.Precision.HIGHEST)
    return (schur_slab, panel_factor)


def solution(mesh):
    split = Mesh(mesh.devices.reshape(mesh.shape["row"], 4, 2), ("row", "col_0", "col_1"))
    placed = (P("row", COL), P("row", None, None), P("row"))
    return jax.shard_map(
        body, mesh=split, in_specs=placed, out_specs=(P("row", COL), P("row", COL)), check_vma=False
    )
```

profile of v0, /device:TPU:49, one launch (start us, length us, event | category | flops | bytes accessed | tf_op | source)
XLA Modules:
  0.0 849.8 jit_solution(13483412741071421629)
XLA Ops:
  7.3 4.9 broadcast_select_fusion
  12.2 15.3 %while.2 = (s32[]{:T(128)}, f32[4,512,512]{2,1,0:T(8,128)}, s32[4,2]{0,1:T(2,128)S(1)}, f32[4,4,128,128]{3,2,0,1:T(8,128)}, s32[]{:T(128)}) while((s32[]{:T(128)}, f32[4,512,512]{2,1,0:T(8,128)}, s32[4,2]{0,1:T(2,128)S(1)}, f32[4,4,128,128]{3,2,0,1:T(8,128)}, s32[]{:T(128)}) %tuple.46), condition=%wide.while_cond, body=%wide.while_body.sunk | while | flops 2 | bytes 525921 | solution.py:28
  12.9 3.2 bitcast_dynamic-update-slice_fusion.4
  16.7 3.2 bitcast_dynamic-update-slice_fusion.4
  20.6 3.2 bitcast_dynamic-update-slice_fusion.4
  24.4 3.1 bitcast_dynamic-update-slice_fusion.4
  27.5 158.0 %custom-call.35 = f32[4,4,128,128]{2,3,1,0:T(8,128)S(1)} custom-call(f32[4,4,128,128]{3,2,1,0:T(8,128)} %bitcast.90), custom_call_target="InvertDiagBlocksLowerTriangular" | custom-call | tf_op jit(solution)/shard_map/vmap(jit(_solve_triangular))/triangular_solve | solution.py:28
  189.8 2.4 fusion.14
  193.2 3.3 fusion.11
  199.8 63.4 %all-gather.7.cloned.1.call-done = bf16[2048,1024]{1,0:T(8,128)(2,1)} async-done(((bf16[2048,512]{1,0:T(8,128)(2,1)}), bf16[2048,1024]{1,0:T(8,128)(2,1)}) %all-gather.7.cloned.1.call-update) | async-done | bytes 4194320 | tf_op jit(solution)/shard_map/all_gather | solution.py:14
  263.3 159.8 %all-gather.9.cloned.1.call-done = bf16[2048,4096]{1,0:T(8,128)(2,1)} async-done(((bf16[2048,1024]{1,0:T(8,128)(2,1)}), bf16[2048,4096]{1,0:T(8,128)(2,1)}) %all-gather.9.cloned.1.call-update) | async-done | bytes 16777232 | tf_op jit(solution)/shard_map/all_gather | solution.py:14
  423.1 14.6 %fusion.69 = f32[4096,512]{0,1:T(8,128)} fusion(bf16[2048,4096]{1,0:T(8,128)(2,1)} %all-gather.9.cloned.1.call-done, bf16[2048,512]{1,0:T(8,128)(2,1)S(1)} %copy-done), kind=kOutput, calls=%fused_computation.115 | convolution fusion | flops 8589934592 | bytes 27262976 | tf_op jit(solution)/shard_map/dot_general | solution.py:41
  437.8 119.9 %reduce-scatter.2.cloned.1.call-done = f32[128,512]{0,1:T(8,128)} async-done(((f32[4096,512]{0,1:T(8,128)}), f32[128,512]{0,1:T(8,128)}) %reduce-scatter.2.cloned.1.call-update) | async-done | bytes 262160 | tf_op jit(solution)/shard_map/reduce_scatter | solution.py:40
  557.8 52.8 %all-gather.11.cloned.1.call-done = f32[1024,512]{0,1:T(8,128)} async-done(((f32[128,512]{0,1:T(8,128)}), f32[1024,512]{0,1:T(8,128)}) %all-gather.11.cloned.1.call-update) | async-done | bytes 2097168 | tf_op jit(solution)/shard_map/all_gather | solution.py:19
  615.0 84.7 %all-gather.13.cloned.1.call-done = f32[4096,512]{0,1:T(8,128)} async-done(((f32[128,512]{0,1:T(8,128)}), f32[4096,512]{0,1:T(8,128)}) %all-gather.13.cloned.1.call-update) | async-done | bytes 8388624 | tf_op jit(solution)/shard_map/all_gather | solution.py:19
  702.9 11.7 %cholesky.104 = f32[128,128]{1,0:T(8,128)S(1)} custom-call(f32[128,128]{1,0:T(8,128)S(1)} %cholesky.266), custom_call_target="Cholesky" | custom-call | tf_op jit(solution)/shard_map/jit(cholesky)/cholesky | solution.py:53
  714.7 9.8 %custom-call.36 = f32[1,128,128]{1,2,0:T(8,128)S(1)} custom-call(f32[1,128,128]{2,1,0:T(8,128)S(1)} %get-tuple-element.49), custom_call_target="InvertDiagBlocksLowerTriangular" | custom-call | tf_op jit(solution)/shard_map/jit(cholesky)/cholesky | solution.py:53
  725.2 11.7 %cholesky.217 = f32[128,128]{1,0:T(8,128)S(1)} custom-call(f32[128,128]{1,0:T(8,128)S(1)} %cholesky.270), custom_call_target="Cholesky" | custom-call | tf_op jit(solution)/shard_map/jit(cholesky)/cholesky | solution.py:53
  737.0 10.0 %custom-call.37 = f32[1,128,128]{1,2,0:T(8,128)S(1)} custom-call(f32[1,128,128]{2,1,0:T(8,128)S(1)} %get-tuple-element.46), custom_call_target="InvertDiagBlocksLowerTriangular" | custom-call | tf_op jit(solution)/shard_map/jit(cholesky)/cholesky | solution.py:53
  747.7 11.7 %cholesky.238 = f32[128,128]{1,0:T(8,128)S(1)} custom-call(f32[128,128]{1,0:T(8,128)S(1)} %cholesky.275), custom_call_target="Cholesky" | custom-call | tf_op jit(solution)/shard_map/jit(cholesky)/cholesky | solution.py:53
  760.1 9.8 %custom-call.38 = f32[1,128,128]{1,2,0:T(8,128)S(1)} custom-call(f32[1,128,128]{2,1,0:T(8,128)S(1)} %get-tuple-element.43), custom_call_target="InvertDiagBlocksLowerTriangular" | custom-call | tf_op jit(solution)/shard_map/jit(cholesky)/cholesky | solution.py:53
  770.5 11.9 %cholesky.255 = f32[128,128]{1,0:T(8,128)S(1)} custom-call(f32[128,128]{1,0:T(8,128)S(1)} %convolution_subtract_fusion.6), custom_call_target="Cholesky" | custom-call | tf_op jit(solution)/shard_map/jit(cholesky)/cholesky | solution.py:53
  786.5 10.5 %while.3 = (s32[]{:T(128)}, f32[512,512]{1,0:T(8,128)S(1)}, s32[4,2]{0,1:T(2,128)S(1)}, f32[4,128,128]{2,1,0:T(8,128)}, s32[]{:T(128)}) while((s32[]{:T(128)}, f32[512,512]{1,0:T(8,128)S(1)}, s32[4,2]{0,1:T(2,128)S(1)}, f32[4,128,128]{2,1,0:T(8,128)}, s32[]{:T(128)}) %tuple.62), condition=%wide.while_cond.1, body=%wide.while_body.1.sunk | while | flops 2 | bytes 132705 | solution.py:54
  797.0 40.1 %custom-call.39 = f32[4,128,128]{1,2,0:T(8,128)S(1)} custom-call(f32[4,128,128]{2,1,0:T(8,128)} %get-tuple-element.17), custom_call_target="InvertDiagBlocksLowerTriangular" | custom-call | tf_op jit(solution)/shard_map/jit(_solve_triangular)/triangular_solve | solution.py:54
  (84 shorter events, 39.6 us)
Async XLA Ops:
  7.2 256.0 %all-gather.7.cloned.1.call-start = ((), (), s32[]{:S(2)}) async-start(), calls=%async_computation.1 | async-start | bytes 6291456 | tf_op jit(solution)/shard_map/all_gather | solution.py:14
  7.3 178.2 %copy-start.1 = (bf16[2048,512]{1,0:T(8,128)(2,1)S(1)}, bf16[2048,512]{1,0:T(8,128)(2,1)}, u32[]{:S(2)}) copy-start(bf16[2048,512]{1,0:T(8,128)(2,1)} %param.3) | copy-start | bytes 6291460
  196.5 1.4 copy-start.2
  199.8 223.3 %copy-start = (bf16[2048,512]{1,0:T(8,128)(2,1)S(1)}, bf16[2048,512]{1,0:T(8,128)(2,1)}, u32[]{:S(2)}) copy-start(bf16[2048,512]{1,0:T(8,128)(2,1)} %fusion) | copy-start | bytes 6291460
  199.8 223.3 %all-gather.9.cloned.1.call-start = ((), (), s32[]{:S(2)}) async-start(), calls=%async_computation.2 | async-start | bytes 20971520 | tf_op jit(solution)/shard_map/all_gather | solution.py:14
  263.2 294.5 %reduce-scatter.2.cloned.1.call-start = ((), (), s32[]{:S(2)}) async-start(), calls=%async_computation.3 | async-start | bytes 8650752 | tf_op jit(solution)/shard_map/reduce_scatter | solution.py:40
  437.8 172.9 %all-gather.11.cloned.1.call-start = ((), (), s32[]{:S(2)}) async-start(), calls=%async_computation.4 | async-start | bytes 2359296 | tf_op jit(solution)/shard_map/all_gather | solution.py:19
  557.8 142.0 %all-gather.13.cloned.1.call-start = ((), (), s32[]{:S(2)}) async-start(), calls=%async_computation.5 | async-start | bytes 8650752 | tf_op jit(solution)/shard_map/all_gather | solution.py:19
Sparse Core Ops, SparseCore 0:
  199.9 63.2 all-gather.6
  265.0 158.0 all-gather.8
  437.9 119.7 reduce-scatter.1
  559.4 51.1 all-gather.10
  613.2 86.4 all-gather.12
where the time goes:
time: 863 us; the launch traced here: 850 us
  waiting for transfers between devices  481 us (56%)
  other arithmetic  287 us (33%)
  matrix products  33.7 us (4%)
  local copies, waits for them, and re-layouts  31 us (4%)
  between operations  17.1 us (2%)
    all_gather x2, waiting for transfers between devices, gathered_by_axis(): nearer = lax.all_gather(value, axes[-1], axis=dim, tiled=True)  223 us
    another operation x5, other arithmetic, whiten(): jax.scipy.linalg.solve_triangular(factor, right, lower=True)  163 us
    all_gather x2, waiting for transfers between devices, picked_2(): lax.all_gather(value, axis)  138 us
    reduce_scatter x1, waiting for transfers between devices, body(): lax.psum_scatter(lax.dot_general(gathered, own_panel, (((0,), (0,)), ((),...  120 us
    another operation x14, other arithmetic, body(): lead_factor = jnp.linalg.cholesky(leading_block)  78.9 us
    another operation x2, other arithmetic, body(): jax.scipy.linalg.solve_triangular(lead_factor, jnp.eye(LEAD, dtype=jnp.fl...  40.2 us
    another operation x24, local copies, waits for them, and re-layouts  25.8 us
  transfers between devices with their start and end apart: 5, of which 5 were waited for; matrix products, arithmetic and copies ran while one was open for 0% of the time, Pallas kernels for 0%

commit v1 on v0

v1 whole, which is shorter than its diff:
```python
import jax
import jax.numpy as jnp
from jax import lax
from jax.experimental import pallas as pl
from jax.experimental.pallas import tpu as pltpu
from jax.sharding import Mesh
from jax.sharding import PartitionSpec as P

HI = lax.Precision.HIGHEST


def dot_f32(a, b):
    return jnp.dot(a, b, precision=HI, preferred_element_type=jnp.float32)


def dot_bf16(a, b):
    return jnp.dot(a, b, preferred_element_type=jnp.float32)


def dot_lhs_t(a, b):
    return lax.dot_general(a, b, (((0,), (0,)), ((), ())), preferred_element_type=jnp.float32)


def three_parts(v):
    high = v.astype(jnp.bfloat16)
    rest = v - high.astype(jnp.float32)
    mid = rest.astype(jnp.bfloat16)
    return high, mid, (rest - mid.astype(jnp.float32)).astype(jnp.bfloat16)


def whiten_block(high, low, segment):
    top = dot_bf16(high[:256, :256], segment[:256]) + dot_bf16(low[:256, :256], segment[:256])
    bottom = dot_bf16(high[256:], segment) + dot_bf16(low[256:], segment)
    return top.astype(jnp.bfloat16), bottom.astype(jnp.bfloat16)


def prepare_kernel(live_ref, factors_ref, blocks_ref, high_ref, low_ref, own_ref, diag_ref,
                   packed, spread, small, wide, inverse):
    row = lax.broadcasted_iota(jnp.int32, (128, 128), 0)
    lane = lax.broadcasted_iota(jnp.int32, (128, 128), 1)
    same = (row // 16) == (lane // 16)
    for f in range(4):
        for d in range(4):
            tile = factors_ref[f, pl.ds(128 * d, 128), pl.ds(128 * d, 128)]
            tile = jnp.where(same, tile, 0.0)
            total = tile[0:16]
            for b in range(1, 8):
                total = total + tile[16 * b:16 * b + 16]
            packed[:, 4 * f + d, :] = total
    high, mid, low = three_parts(packed[...].reshape(256, 128))
    for j in range(16):
        pick = jnp.where(same & (row % 16 == j), 1.0, 0.0).astype(jnp.bfloat16)
        spread[j] = (dot_bf16(high, pick) + dot_bf16(mid, pick) + dot_bf16(low, pick)).reshape(16, 16, 128)
    lane16 = lax.broadcasted_iota(jnp.int32, (16, 128), 1) % 16
    rows = []
    for i in range(16):
        value = jnp.where(lane16 == i, 1.0, 0.0)
        for j in range(i):
            value = value - spread[j, i] * rows[j]
        value = value / spread[i, i]
        rows.append(value)
        small[i] = value
    row2 = lax.broadcasted_iota(jnp.int32, (256, 256), 0)
    lane2 = lax.broadcasted_iota(jnp.int32, (256, 256), 1)

    def grow(block, _):
        f, h = block // 2, block % 2
        tile = factors_ref[f, pl.ds(pl.multiple_of(256 * h, 256), 256), pl.ds(pl.multiple_of(256 * h, 256), 256)]
        for d in range(2):
            narrow = small[:, 2 * block + d, :]
            wide[pl.ds(128 * d, 128), :] = jnp.where(same, jnp.concatenate([narrow] * 8, axis=0), 0.0)
        zero = jnp.zeros((128, 128), jnp.float32)
        held = jnp.concatenate([
            jnp.concatenate([wide[0:128, :], zero], axis=1),
            jnp.concatenate([zero, wide[128:256, :]], axis=1)], axis=0)
        for s in (16, 32, 64, 128):
            mask = ((row2 // (2 * s)) == (lane2 // (2 * s))) & (row2 % (2 * s) >= s) & (lane2 % (2 * s) < s)
            cross = jnp.where(mask, tile, 0.0)
            lower = [slice(2 * s * g + s, 2 * s * g + 2 * s) for g in range(256 // (2 * s))]
            odd = lambda v: jnp.concatenate([v[sl] for sl in lower], axis=0)
            first = dot_f32(odd(cross), held)
            pieces = []
            for g in range(256 // (2 * s)):
                pieces.append(jnp.zeros((s, 256), jnp.float32))
                pieces.append(first[g * s:(g + 1) * s])
            second = dot_f32(odd(held), jnp.concatenate(pieces, axis=0))
            pieces = []
            for g in range(256 // (2 * s)):
                pieces.append(held[2 * s * g:2 * s * g + s])
                pieces.append(held[2 * s * g + s:2 * s * g + 2 * s] - second[g * s:(g + 1) * s])
            held = jnp.concatenate(pieces, axis=0)
        inverse[block] = held
        return _

    lax.fori_loop(0, 8, grow, 0)

    def finish(f, _):
        live = live_ref[f]
        first, last = inverse[2 * f], inverse[2 * f + 1]
        corner = -dot_f32(last, dot_f32(factors_ref[f, 256:512, 0:256], first))

        def put(value, r, c):
            index = lax.broadcasted_iota(jnp.int32, (256, 256), 0) + r
            value = jnp.where(index < live, value, 0.0)
            high = value.astype(jnp.bfloat16)
            high_ref[f, r:r + 256, c:c + 256] = high
            low_ref[f, r:r + 256, c:c + 256] = (value - high.astype(jnp.float32)).astype(jnp.bfloat16)

        put(first, 0, 0)
        put(corner, 256, 0)
        put(last, 256, 256)
        put(jnp.zeros((256, 256), jnp.float32), 0, 256)
        start = pl.multiple_of(512 * f, 512)
        top, bottom = whiten_block(high_ref[f], low_ref[f], blocks_ref[pl.ds(start, 512), :])
        own_ref[pl.ds(start, 256), :] = top
        own_ref[pl.ds(start + 256, 256), :] = bottom
        return _

    lax.fori_loop(0, 4, finish, 0)
    diag_ref[...] = dot_lhs_t(own_ref[...], own_ref[...])


def prepare(blocks, factors, live):
    vmem = pl.BlockSpec(memory_space=pltpu.VMEM)
    return pl.pallas_call(
        prepare_kernel,
        out_shape=(
            jax.ShapeDtypeStruct((4, 512, 512), jnp.bfloat16),
            jax.ShapeDtypeStruct((4, 512, 512), jnp.bfloat16),
            jax.ShapeDtypeStruct((2048, 512), jnp.bfloat16),
            jax.ShapeDtypeStruct((512, 512), jnp.float32),
        ),
        in_specs=[pl.BlockSpec(memory_space=pltpu.SMEM), vmem, vmem],
        out_specs=(vmem,) * 4,
        scratch_shapes=[
            pltpu.VMEM((16, 16, 128), jnp.float32),
            pltpu.VMEM((16, 16, 16, 128), jnp.float32),
            pltpu.VMEM((16, 16, 128), jnp.float32),
            pltpu.VMEM((256, 128), jnp.float32),
            pltpu.VMEM((8, 256, 256), jnp.float32),
        ],
        compiler_params=pltpu.CompilerParams(vmem_limit_bytes=48 << 20),
        cost_estimate=pl.CostEstimate(flops=16 << 30, bytes_accessed=14 << 20, transcendentals=0),
    )(live, factors, blocks)


def lead_kernel(lead_ref, out_ref, work, parts):
    work[...] = lead_ref[...]
    row = lax.broadcasted_iota(jnp.int32, (128, 128), 0)
    lane = lax.broadcasted_iota(jnp.int32, (128, 128), 1)
    sub = lax.broadcasted_iota(jnp.int32, (8, 128), 0)
    lan = lax.broadcasted_iota(jnp.int32, (8, 128), 1)

    def factor(p):
        base = 128 * p
        a = [work[base + 8 * g:base + 8 * g + 8, base:base + 128] for g in range(16)]
        x = [jnp.where(sub + 8 * g == lan, 1.0, 0.0) for g in range(16)]
        scale = []
        for k in range(128):
            g0, s0 = k // 8, k % 8
            arow = a[g0][s0:s0 + 1, :]
            xrow = x[g0][s0:s0 + 1, :]
            pivot = arow[:, k:k + 1]
            inv = 1.0 / pivot
            scale.append(pivot)
            arow_n = arow * inv
            xrow_n = xrow * inv
            for g in range(g0, 16):
                col = a[g][:, k:k + 1]
                if g == g0:
                    if s0 == 7:
                        continue
                    col = jnp.where(sub[:, :1] > s0, col, 0.0)
                if k < 127:
                    a[g] = a[g] - col * arow_n
                    x[g] = x[g] - col * xrow_n
        pivots = jnp.concatenate(scale, axis=0)
        whole = jnp.concatenate(x, axis=0)
        return whole * lax.rsqrt(pivots)

    for p in range(4):
        own = factor(p)
        parts[p] = own
        if p < 3:
            rest = 128 * (3 - p)
            base = 128 * p + 128
            below = work[base:512, base - 128:base]
            panel = lax.dot_general(below, own, (((1,), (1,)), ((), ())), precision=HI, preferred_element_type=jnp.float32)
            work[base:512, base - 128:base] = panel
            work[base:512, base:512] = work[base:512, base:512] - lax.dot_general(
                panel, panel, (((1,), (1,)), ((), ())), precision=HI, preferred_element_type=jnp.float32)
    zero = jnp.zeros((128, 128), jnp.float32)
    out_ref[0:256, 256:512] = jnp.zeros((256, 256), jnp.float32)
    for h in range(2):
        o = 256 * h
        first, last = parts[2 * h], parts[2 * h + 1]
        out_ref[o:o + 128, o:o + 128] = first
        out_ref[o:o + 128, o + 128:o + 256] = zero
        out_ref[o + 128:o + 256, o + 128:o + 256] = last
        out_ref[o + 128:o + 256, o:o + 128] = -dot_f32(last, dot_f32(work[o + 128:o + 256, o:o + 128], first))
    out_ref[256:512, 0:256] = -dot_f32(
        out_ref[256:512, 256:512], dot_f32(work[256:512, 0:256], out_ref[0:256, 0:256]))


def lead_inverse_of(lead):
    vmem = pl.BlockSpec(memory_space=pltpu.VMEM)
    return pl.pallas_call(
        lead_kernel,
        out_shape=jax.ShapeDtypeStruct((512, 512), jnp.float32),
        in_specs=[vmem],
        out_specs=vmem,
        scratch_shapes=[pltpu.VMEM((512, 512), jnp.float32), pltpu.VMEM((4, 128, 128), jnp.float32)],
        compiler_params=pltpu.CompilerParams(vmem_limit_bytes=24 << 20),
        cost_estimate=pl.CostEstimate(flops=40 << 30, bytes_accessed=2 << 20, transcendentals=0),
    )(lead)


AXES = ("y", "zh", "k", "x", "zl")
MESH = pl.DeviceIdType.MESH


def tiles_kernel(high_ref, low_ref, own_ref, near_ref, next_ref, far_ref, out_ref, pair, side, half):
    x, z = lax.axis_index("x"), lax.axis_index("zl")
    own_at, near_at = pl.multiple_of(512 * z, 512), pl.multiple_of(512 - 512 * z, 512)
    h = x // 2

    def whiten(f, _):
        start = pl.multiple_of(512 * f, 512)
        rows = pl.ds(start, 512)
        pair[rows, pl.ds(own_at, 512)] = own_ref[rows, :]
        high, low = high_ref[f], low_ref[f]
        top, bottom = whiten_block(high, low, near_ref[rows, :])
        pair[pl.ds(start, 256), pl.ds(near_at, 512)] = top
        pair[pl.ds(start + 256, 256), pl.ds(near_at, 512)] = bottom
        top, bottom = whiten_block(high, low, next_ref[rows, :])
        side[pl.ds(start, 256), :] = top
        side[pl.ds(start + 256, 256), :] = bottom
        return _

    lax.fori_loop(0, 4, whiten, 0)
    for f in range(2):
        top, bottom = whiten_block(high_ref[2 * h + f], low_ref[2 * h + f], far_ref[512 * f:512 * f + 512, :])
        half[512 * f:512 * f + 256, :] = top
        half[512 * f + 256:512 * f + 512, :] = bottom
    for p in range(2):
        for n in range(4):
            cols = slice(256 * n, 256 * n + 256)
            one = dot_lhs_t(side[:, 256 * p:256 * p + 256], pair[:, cols]).astype(jnp.bfloat16)
            two = dot_lhs_t(half[:, 256 * p:256 * p + 256], pair[pl.ds(pl.multiple_of(1024 * h, 1024), 1024), cols]).astype(jnp.bfloat16)
            for i in range(2):
                for j in range(2):
                    a, b = 2 * p + i, 2 * n + j
                    at = (1 - a % 2, 2 * (a // 2) + b % 2, b // 2)
                    out_ref[at[0], at[1], at[2], 0:128, :] = one[128 * i:128 * i + 128, 128 * j:128 * j + 128]
                    out_ref[at[0], at[1], at[2], 128:256, :] = two[128 * i:128 * i + 128, 128 * j:128 * j + 128]
    lhs = pair[:, pl.ds(pl.multiple_of(256 * z, 256), 256)]
    for n in range(2):
        zt = dot_lhs_t(lhs, pair[:, 512 + 256 * n:768 + 256 * n]).astype(jnp.bfloat16)
        for i in range(2):
            for j in range(2):
                b = 2 * n + j
                for s in range(4):
                    out_ref[1 - i, s, (b + 3) % 4, 256:288, :] = zt[128 * i + 32 * s:128 * i + 32 * s + 32, 128 * j:128 * j + 128]


def tiles(high, low, own, near, nxt, far):
    vmem = pl.BlockSpec(memory_space=pltpu.VMEM)
    return pl.pallas_call(
        tiles_kernel,
        out_shape=jax.ShapeDtypeStruct((2, 4, 4, 288, 128), jnp.bfloat16),
        in_specs=[vmem] * 6,
        out_specs=vmem,
        scratch_shapes=[
            pltpu.VMEM((2048, 1024), jnp.bfloat16),
            pltpu.VMEM((2048, 512), jnp.bfloat16),
            pltpu.VMEM((1024, 512), jnp.bfloat16),
        ],
        compiler_params=pltpu.CompilerParams(vmem_limit_bytes=48 << 20),
        cost_estimate=pl.CostEstimate(flops=14 << 30, bytes_accessed=14 << 20, transcendentals=0),
    )(high, low, own, near, nxt, far)


def remote(src, dst, send, recv, **where):
    return pltpu.make_async_remote_copy(
        src_ref=src, dst_ref=dst, send_sem=send, recv_sem=recv, device_id=where, device_id_type=MESH)


def wrapped(i):
    return lax.rem(i + 8, 4)


def greet(barrier, **where):
    pl.semaphore_signal(barrier, inc=1, device_id=where, device_id_type=MESH)


def row_partners(barrier, y, zh, k):
    greet(barrier, k=1 - k)
    for d in range(1, 4):
        greet(barrier, y=wrapped(y + d))
        greet(barrier, zh=wrapped(zh + d))


def lead_sum_kernel(in_ref, out_ref, from_k, part_k, from_y, part_y, from_zh, whole, send, recv):
    y, zh, k = lax.axis_index("y"), lax.axis_index("zh"), lax.axis_index("k")
    barrier = pltpu.get_barrier_semaphore()
    row_partners(barrier, y, zh, k)
    pl.semaphore_wait(barrier, 7)
    copy = remote(in_ref.at[1 - k], from_k, send.at[0], recv.at[0], k=1 - k)
    copy.start()
    copy.wait()
    part_k[...] = in_ref[k] + from_k[...]
    copies = []
    for d in range(1, 4):
        copy = remote(part_k.at[wrapped(y + d)], from_y.at[d - 1], send.at[d], recv.at[d], y=wrapped(y + d))
        copy.start()
        copies.append(copy)
    for copy in copies:
        copy.wait()
    part_y[...] = part_k[y] + from_y[0] + from_y[1] + from_y[2]
    copies = []
    for d in range(1, 4):
        copy = remote(part_y.at[wrapped(zh + d)], from_zh.at[d - 1], send.at[3 + d], recv.at[3 + d], zh=wrapped(zh + d))
        copy.start()
        copies.append(copy)
    for copy in copies:
        copy.wait()
    whole[k, y, zh] = part_y[zh] + from_zh[0] + from_zh[1] + from_zh[2]
    copies = []
    for d in range(1, 4):
        mine = whole.at[k, y, zh]
        copy = remote(mine, mine, send.at[6 + d], recv.at[6 + d], zh=wrapped(zh + d))
        copy.start()
        copies.append(copy)
    for copy in copies:
        copy.wait()
    copies = []
    for d in range(1, 4):
        mine = whole.at[k, y]
        copy = remote(mine, mine, send.at[9 + d], recv.at[9 + d], y=wrapped(y + d))
        copy.start()
        copies.append(copy)
    for copy in copies:
        copy.wait()
    copy = remote(whole.at[k], whole.at[k], send.at[13], recv.at[13], k=1 - k)
    copy.start()
    copy.wait()
    out_ref[...] = whole[...]


def lead_sum(diag):
    vmem = pl.BlockSpec(memory_space=pltpu.VMEM)
    f32 = jnp.float32
    return pl.pallas_call(
        lead_sum_kernel,
        out_shape=jax.ShapeDtypeStruct((2, 4, 4, 16, 512), f32),
        in_specs=[vmem],
        out_specs=vmem,
        scratch_shapes=[
            pltpu.VMEM((4, 4, 16, 512), f32),
            pltpu.VMEM((4, 4, 16, 512), f32),
            pltpu.VMEM((3, 4, 16, 512), f32),
            pltpu.VMEM((4, 16, 512), f32),
            pltpu.VMEM((3, 16, 512), f32),
            pltpu.VMEM((2, 4, 4, 16, 512), f32),
            pltpu.SemaphoreType.DMA((14,)),
            pltpu.SemaphoreType.DMA((14,)),
        ],
        compiler_params=pltpu.CompilerParams(
            vmem_limit_bytes=24 << 20, collective_id=0, has_side_effects=True),
        cost_estimate=pl.CostEstimate(flops=20 << 30, bytes_accessed=2 << 20, transcendentals=0),
    )(diag.reshape(2, 4, 4, 16, 512)).reshape(512, 512)


def spread_kernel(parts_ref, lead_ref, inverse_ref, out_ref, panel_ref,
                  from_k, part_k, from_y, part_y, from_zh, final, land, land_t, strips, strip_in,
                  send, recv, land_sem, land_t_sem, strip_sem, strip_send, panel_sem):
    y, zh, k = lax.axis_index("y"), lax.axis_index("zh"), lax.axis_index("k")
    x, z = lax.axis_index("x"), lax.axis_index("zl")
    f32 = jnp.float32
    leader = (x == 0) & (z == 0)
    zr, q = zh // 2, 2 * lax.rem(zh, 2) + k
    dx = wrapped(y - x)
    is_direct = (dx == 1) | (dx == 2)
    is_turned = (dx == 3) | (dx == 2)
    strip_direct = (dx == 0) & (zr == 0) & (z == 1)
    strip_turned = (dx == 0) & (zr == 1) & (z == 0)
    is_diag = (dx == 0) & (zr == z)

    barrier = pltpu.get_barrier_semaphore()
    row_partners(barrier, y, zh, k)

    @pl.when(is_direct)
    def _():
        for j in range(4):
            b = 4 * z + j
            greet(barrier, k=1 - lax.rem(q, 2), y=2 * (q // 2) + lax.rem(b, 2), zh=b // 2, x=x, zl=zr)

    @pl.when(is_turned)
    def _():
        for j in range(4):
            greet(barrier, k=1 - j % 2, y=2 * (j // 2) + k, zh=zh, x=y, zl=z)

    @pl.when(strip_direct)
    def _():
        for j in range(4):
            for s in range(4):
                greet(barrier, k=1 - k, y=s, zh=(j + 3) % 4, x=x, zl=zh)

    @pl.when(strip_turned)
    def _():
        for j in range(4):
            for s in range(4):
                greet(barrier, k=1 - j % 2, y=s, zh=lax.rem(2 * (zh - 2) + k + 3, 4), x=x, zl=j // 2)

    @pl.when(leader)
    def _():
        pl.semaphore_wait(barrier, 20)

    @pl.when(jnp.logical_not(leader))
    def _():
        greet(barrier, x=0, zl=0)
        pl.semaphore_wait(barrier, 13)

    copy = remote(parts_ref.at[1 - k], from_k, send.at[0], recv.at[0], k=1 - k)
    copy.start()
    copy.wait()
    for i in range(4):
        part_k[i] = (parts_ref[k, i].astype(f32) + from_k[i].astype(f32)).astype(jnp.bfloat16)
    copies = []
    for d in range(1, 4):
        copy = remote(part_k.at[wrapped(y + d)], from_y.at[d - 1], send.at[d], recv.at[d], y=wrapped(y + d))
        copy.start()
        copies.append(copy)
    for copy in copies:
        copy.wait()
    part_y[...] = ((part_k[y].astype(f32) + from_y[0].astype(f32)) + (from_y[1].astype(f32) + from_y[2].astype(f32))).astype(jnp.bfloat16)
    copies = []
    for d in range(1, 4):
        copy = remote(part_y.at[wrapped(zh + d)], from_zh.at[d - 1], send.at[3 + d], recv.at[3 + d], zh=wrapped(zh + d))
        copy.start()
        copies.append(copy)
    for copy in copies:
        copy.wait()
    final[...] = (part_y[zh].astype(f32) + from_zh[0].astype(f32)) + (from_zh[1].astype(f32) + from_zh[2].astype(f32))

    a, b = 2 * (y // 2) + 1 - k, 2 * zh + lax.rem(y, 2)
    a2, b2 = 1 - k, wrapped(zh + 1)
    one, two, strip = final.at[pl.ds(0, 128)], final.at[pl.ds(128, 128)], final.at[pl.ds(256, 32)]
    sent = [
        remote(one, land.at[lax.rem(b, 4)], send.at[7], land_sem.at[lax.rem(b, 4)],
               x=x, zl=b // 4, y=wrapped(x + 1), zh=2 * z + a // 2, k=lax.rem(a, 2)),
        remote(one, land.at[a], send.at[8], land_sem.at[a],
               x=wrapped(x + 1), zl=z, y=x, zh=b // 2, k=lax.rem(b, 2)),
        remote(two, land.at[lax.rem(b, 4)], send.at[9], land_sem.at[lax.rem(b, 4)],
               x=x, zl=b // 4, y=wrapped(x + 2), zh=2 * z + a // 2, k=lax.rem(a, 2)),
        remote(two, land_t.at[a], send.at[10], land_t_sem.at[a],
               x=wrapped(x + 2), zl=z, y=x, zh=b // 2, k=lax.rem(b, 2)),
        remote(strip, strips.at[b2, y], strip_send.at[0], strip_sem.at[4 * b2 + y],
               x=x, zl=1, y=x, zh=z, k=a2),
        remote(strip, strips.at[2 * z + a2, y], strip_send.at[1], strip_sem.at[4 * (2 * z + a2) + y],
               x=x, zl=0, y=x, zh=2 + b2 // 2, k=lax.rem(b2, 2)),
    ]
    for copy in sent:
        copy.start()

    def arrived(j):
        remote(one, land.at[j], send.at[7], land_sem.at[j], k=1 - k).wait_recv()

    def arrived_turned(j):
        remote(one, land_t.at[j], send.at[7], land_t_sem.at[j], k=1 - k).wait_recv()

    def arrived_strips(j):
        for s in range(4):
            remote(strip, strips.at[j, s], strip_send.at[0], strip_sem.at[4 * j + s], k=1 - k).wait_recv()
        return jnp.concatenate([strips[j, s] for s in range(4)], axis=0)

    @pl.when(is_diag)
    def _():
        out_ref[...] = lead_ref[pl.ds(pl.multiple_of(128 * q, 128), 128), :]

    @pl.when(dx == 1)
    def _():
        for j in range(4):
            arrived(j)
            out_ref[:, 128 * j:128 * j + 128] = land[j]

    @pl.when(dx == 3)
    def _():
        for j in range(4):
            arrived(j)
            out_ref[:, 128 * j:128 * j + 128] = land[j].T

    @pl.when(dx == 2)
    def _():
        for j in range(4):
            arrived(j)
            arrived_turned(j)
            out_ref[:, 128 * j:128 * j + 128] = land[j] + land_t[j].T

    @pl.when(strip_direct)
    def _():
        for j in range(4):
            out_ref[:, 128 * j:128 * j + 128] = arrived_strips(j)

    @pl.when(strip_turned)
    def _():
        for j in range(4):
            out_ref[:, 128 * j:128 * j + 128] = arrived_strips(j).T

    @pl.when(leader)
    def _():
        slab = out_ref[...]
        for c in range(8):
            strip_in[c] = lax.dot_general(
                slab, inverse_ref[64 * c:64 * c + 64, :], (((1,), (1,)), ((), ())), precision=HI, preferred_element_type=f32)
            if c:
                remote(strip_in.at[c], strip_in.at[0], panel_sem.at[c], panel_sem.at[0], x=c // 2, zl=c % 2).start()
        panel_ref[...] = strip_in[0]
        for c in range(1, 8):
            remote(strip_in.at[c], strip_in.at[0], panel_sem.at[c], panel_sem.at[0], x=c // 2, zl=c % 2).wait_send()

    @pl.when(jnp.logical_not(leader))
    def _():
        remote(strip_in.at[1], strip_in.at[0], panel_sem.at[1], panel_sem.at[0], k=1 - k).wait_recv()
        panel_ref[...] = strip_in[0]

    for copy in sent:
        copy.wait_send()


def spread(parts, lead, inverse):
    vmem = pl.BlockSpec(memory_space=pltpu.VMEM)
    f32, bf16 = jnp.float32, jnp.bfloat16
    dma = pltpu.SemaphoreType.DMA
    return pl.pallas_call(
        spread_kernel,
        out_shape=(jax.ShapeDtypeStruct((128, 512), f32), jax.ShapeDtypeStruct((128, 64), f32)),
        in_specs=[vmem] * 3,
        out_specs=(vmem, vmem),
        scratch_shapes=[
            pltpu.VMEM((4, 4, 288, 128), bf16),
            pltpu.VMEM((4, 4, 288, 128), bf16),
            pltpu.VMEM((3, 4, 288, 128), bf16),
            pltpu.VMEM((4, 288, 128), bf16),
            pltpu.VMEM((3, 288, 128), bf16),
            pltpu.VMEM((288, 128), f32),
            pltpu.VMEM((4, 128, 128), f32),
            pltpu.VMEM((4, 128, 128), f32),
            pltpu.VMEM((4, 4, 32, 128), f32),
            pltpu.VMEM((8, 128, 64), f32),
            dma((11,)), dma((7,)), dma((4,)), dma((4,)), dma((16,)), dma((2,)), dma((8,)),
        ],
        compiler_params=pltpu.CompilerParams(
            vmem_limit_bytes=32 << 20, collective_id=1, has_side_effects=True),
        cost_estimate=pl.CostEstimate(flops=20 << 30, bytes_accessed=4 << 20, transcendentals=0),
    )(parts, lead, inverse)


def shifted(value, axis, step, size):
    return lax.ppermute(value, axis, [(i, (i + step) % size) for i in range(size)])


def body(blocks, factors, block_live):
    x = lax.axis_index("x")
    outgoing = lax.dynamic_slice_in_dim(blocks, 1024 * (1 - x // 2), 1024, 0)
    far = shifted(shifted(outgoing, "x", 1, 4), "x", 1, 4)
    near = shifted(blocks, "zl", 1, 2)
    nxt = shifted(blocks, "x", -1, 4)
    high, low, own, diag = prepare(blocks, factors, block_live)
    lead = lead_sum(diag)
    inverse = lead_inverse_of(lead)
    near, nxt, far, inverse = lax.optimization_barrier((near, nxt, far, inverse))
    parts = tiles(high, low, own, near, nxt, far)
    return spread(parts, lead, inverse)


def solution(mesh):
    split = Mesh(mesh.devices.reshape(4, 4, 2, 4, 2), AXES)
    row, col = ("y", "zh", "k"), ("x", "zl")
    return jax.shard_map(
        body, mesh=split, in_specs=(P(row, col), P(row, None, None), P(row)),
        out_specs=(P(row, col), P(row, col)), check_vma=False)
```

time: 863 us -> 190 us (0.22); the launches traced: 850 us -> 186 us
  waiting for transfers between devices: 481 us -> 0.01 us
  other arithmetic: 287 us -> 0 us
  Pallas kernels: 0 us -> 176 us
  matrix products: 33.7 us -> 0 us
  local copies, waits for them, and re-layouts: 31 us -> 5.71 us
  between operations: 17.1 us -> 0.73 us
    all_gather x4 -> x0, waiting for transfers between devices: 361 us -> none  [the longest x2 223 us: gathered_by_axis(): nearer = lax.all_gather(value, axes[-1], axis=dim, tiled=True)]
    another operation x21 -> x0, other arithmetic: 282 us -> none  [the longest x5 163 us: whiten(): jax.scipy.linalg.solve_triangular(factor, right, lower=True)]
    pallas_call x0 -> x5, Pallas kernels: none -> 176 us  [the longest x1 46.9 us: spread(): pl.pallas_call(spread_kernel, out_shape=(jax.ShapeDtypeStruct((128, 512),...]
    reduce_scatter x1 -> x0, waiting for transfers between devices: 120 us -> none  [body(): lax.psum_scatter(lax.dot_general(gathered, own_panel, (((0,), (0,)), ((),...]
    another operation x29 -> x0, local copies, waits for them, and re-layouts: 25.9 us -> none
    another operation x20 -> x0, matrix products: 17.1 us -> none  [the longest x7 11.5 us: whiten(): jax.scipy.linalg.solve_triangular(factor, right, lower=True)]
    dot_general x2 -> x0, matrix products: 16.5 us -> none  [the longest x1 14.6 us: body(): lax.dot_general(gathered, own_panel, (((0,), (0,)), ((), ())), preferred_...]
  transfers between devices with their start and end apart: 5 -> 4, of which waited for: 5 -> 0; matrix products, arithmetic and copies ran while one was open for 0% -> 1% of each run, Pallas kernels for 0% -> 62%
where the time goes in v1:
time: 190 us; the launch traced here: 186 us
  Pallas kernels  176 us (93%)
  local copies, waits for them, and re-layouts  5.71 us (3%)
  starting transfers between devices  3.45 us (2%)
    pallas_call x1, Pallas kernels, spread(): pl.pallas_call(spread_kernel, out_shape=(jax.ShapeDtypeStruct((128, 512),...  46.9 us
    pallas_call x1, Pallas kernels, lead_inverse_of(): pl.pallas_call(lead_kernel, out_shape=jax.ShapeDtypeStruct((512, 512), jn...  46.5 us
    pallas_call x1, Pallas kernels, lead_sum(): pl.pallas_call(lead_sum_kernel, out_shape=jax.ShapeDtypeStruct((2, 4, 4,...  37.2 us
    pallas_call x1, Pallas kernels, prepare(): pl.pallas_call(prepare_kernel, out_shape=(jax.ShapeDtypeStruct((4, 512, 5...  32.3 us
    pallas_call x1, Pallas kernels, tiles(): pl.pallas_call(tiles_kernel, out_shape=jax.ShapeDtypeStruct((2, 4, 4, 288...  13.1 us
  transfers between devices with their start and end apart: 4, of which 0 were waited for; matrix products, arithmetic and copies ran while one was open for 1% of the time, Pallas kernels for 62%

profile of v1, /device:TPU:49, one launch (start us, length us, event | category | flops | bytes accessed | tf_op | source)
XLA Modules:
  0.0 186.0 jit_solution(13812647820308981606)
XLA Ops:
  0.6 0.0 copy-start
  0.6 0.1 collective-permute-start
  0.7 2.6 %collective-permute-start.1 = (bf16[2048,512]{1,0:T(8,128)(2,1)}, bf16[2048,512]{1,0:T(8,128)(2,1)}, u32[]{:S(2)}, u32[]{:S(2)}) collective-permute-start(bf16[2048,512]{1,0:T(8,128)(2,1)} %blocks_ref.1), channel_id=1, source_target_pairs={{0,6},{2,0},{4,2},{6,4},{1,7},{3,1},{5,3},{7,5},{8,14},{10,8},{12,... | collective-permute-start | bytes 6291464 | tf_op jit(solution)/shard_map/ppermute | solution.py:560
  3.3 1.3 constant_dynamic-slice_fusion
  4.6 0.1 collective-permute-start.2
  4.7 0.0 copy-done
  4.7 32.3 %shard_map.50 = (bf16[4,512,512]{2,1,0:T(8,128)(2,1)S(1)}, bf16[4,512,512]{2,1,0:T(8,128)(2,1)S(1)}, bf16[2048,512]{1,0:T(8,128)(2,1)}, f32[512,512]{1,0:T(8,128)S(1)}) custom-call(s32[4]{0:T(128)S(1)} %copy-done, f32[4,512,512]{2,1,0:T(8,128)} %factors_ref.1, bf16[2048,512]{1,0:T(8,128)(2,1)} %blocks_ref.1), custom_call_target="tpu_custom_call" | custom-call | flops 17179869184 | bytes 14680064 | tf_op jit(solution)/shard_map/pallas_call | solution.py:125
  37.0 37.2 %shard_map.51 = f32[2,4,4,16,512]{4,3,2,1,0:T(8,128)S(1)} custom-call(f32[2,4,4,16,512]{4,3,2,1,0:T(8,128)S(1)} %bitcast.4), custom_call_target="tpu_custom_call" | custom-call | flops 21474836480 | bytes 2097152 | tf_op jit(solution)/shard_map/pallas_call | solution.py:353
  74.2 0.0 collective-permute-done.2
  74.2 0.7 collective-permute-start.3
  75.0 46.5 %shard_map.52.inverse_ref = f32[512,512]{1,0:T(8,128)S(1)} custom-call(f32[512,512]{1,0:T(8,128)S(1)} %bitcast.2), custom_call_target="tpu_custom_call" | custom-call | flops 42949672960 | bytes 2097152 | tf_op jit(solution)/shard_map/pallas_call | solution.py:207
  121.5 0.0 collective-permute-done.3.far_ref
  121.5 0.0 collective-permute-done.near_ref
  121.5 0.0 copy-start.2
  121.5 0.0 collective-permute-done.1.next_ref
  121.6 1.3 copy-done.2
  122.9 13.1 %shard_map.53.parts_ref = bf16[2,4,4,288,128]{4,3,2,1,0:T(8,128)(2,1)} custom-call(bf16[4,512,512]{2,1,0:T(8,128)(2,1)S(1)} %get-tuple-element.10.high_ref, bf16[4,512,512]{2,1,0:T(8,128)(2,1)S(1)} %get-tuple-element.11.low_ref, bf16[2048,512]{1,0:T(8,128)(2,1)} %get-tuple-element.12.own_ref, bf16[2048,512]{1,0:T(8,128)(2,1)} %copy-done.2, ...), custom_call_target="tpu_custom_call" | custom-call | flops 15032385536 | bytes 14680064 | tf_op jit(solution)/shard_map/pallas_call | solution.py:268
  136.0 0.0 copy-start.1
  136.0 1.7 copy-done.1
  137.7 46.9 %shard_map.54 = (f32[128,512]{1,0:T(8,128)S(1)}, f32[128,64]{1,0:T(8,128)S(1)}) custom-call(bf16[2,4,4,288,128]{4,3,2,1,0:T(8,128)(2,1)S(1)} %copy-done.1, f32[512,512]{1,0:T(8,128)S(1)} %bitcast.3, f32[512,512]{1,0:T(8,128)S(1)} %shard_map.52.inverse_ref), custom_call_target="tpu_custom_call" | custom-call | flops 21474836480 | bytes 4194304 | tf_op jit(solution)/shard_map/pallas_call | solution.py:535
  184.6 0.7 copy.5
  185.3 0.7 copy.7
Async XLA Ops:
  0.6 4.1 %copy-start = (s32[4]{0:T(128)S(1)}, s32[4]{0:T(128)}, u32[]{:S(2)}) copy-start(s32[4]{0:T(128)} %live_ref.1) | copy-start | bytes 52
  0.6 120.9 %collective-permute-start = (bf16[2048,512]{1,0:T(8,128)(2,1)}, bf16[2048,512]{1,0:T(8,128)(2,1)S(1)}, u32[]{:S(2)}, u32[]{:S(2)}) collective-permute-start(bf16[2048,512]{1,0:T(8,128)(2,1)} %blocks_ref.1), channel_id=1, source_target_pairs={{0,1},{1,0},{2,3},{3,2},{4,5},{5,4},{6,7},{7,6},{8,9},{9,8},{10,11... | collective-permute-start | bytes 6291464 | tf_op jit(solution)/shard_map/ppermute | solution.py:560
  0.7 120.8 %collective-permute-start.1 = (bf16[2048,512]{1,0:T(8,128)(2,1)}, bf16[2048,512]{1,0:T(8,128)(2,1)}, u32[]{:S(2)}, u32[]{:S(2)}) collective-permute-start(bf16[2048,512]{1,0:T(8,128)(2,1)} %blocks_ref.1), channel_id=1, source_target_pairs={{0,6},{2,0},{4,2},{6,4},{1,7},{3,1},{5,3},{7,5},{8,14},{10,8},{12,... | collective-permute-start | bytes 6291464 | tf_op jit(solution)/shard_map/ppermute | solution.py:560
  4.6 69.6 %collective-permute-start.2 = (bf16[1024,512]{1,0:T(8,128)(2,1)S(1)}, bf16[1024,512]{1,0:T(8,128)(2,1)S(1)}, u32[]{:S(2)}, u32[]{:S(2)}) collective-permute-start(bf16[1024,512]{1,0:T(8,128)(2,1)S(1)} %constant_dynamic-slice_fusion), channel_id=1, source_target_pairs={{0,2},{2,4},{4,6},{6,0},{1,3},{3,5},{5,7},{7,1},{8,10},{10,12},{12... | collective-permute-start | bytes 3145736 | tf_op jit(solution)/shard_map/ppermute | solution.py:560
  74.2 47.3 %collective-permute-start.3 = (bf16[1024,512]{1,0:T(8,128)(2,1)S(1)}, bf16[1024,512]{1,0:T(8,128)(2,1)S(1)}, u32[]{:S(2)}, u32[]{:S(2)}) collective-permute-start(bf16[1024,512]{1,0:T(8,128)(2,1)S(1)} %collective-permute-done.2), channel_id=1, source_target_pairs={{0,2},{2,4},{4,6},{6,0},{1,3},{3,5},{5,7},{7,1},{8,10},{10,12},{12... | collective-permute-start | bytes 3145736 | tf_op jit(solution)/shard_map/ppermute | solution.py:560
  121.5 1.3 copy-start.2
  136.0 1.7 copy-start.1
